TPU v7x, 32 devices: a whole 2x2x4 slice. The times are simulated.
32 devices in a mesh: parts: 2 (over y), row: 4 (over z), col: 2 (over x), sub: 2 (over core).
Axes of the slice: x: 2, y: 2, z: 4, core: 2. Of those that a mesh axis runs over, the one named last changes fastest.
Arguments:
- ancestor_cov: float32 [64, 32, 256, 256], P(('parts', 'row'), 'col'), parts along dimension 0, may hold values from -6 to 6
- owner_slot: int32 [64], P('parts'), parts along dimension 0, may hold values from 0 to 31, each once
- parent_pattern: int32 [8, 12], P(('parts', 'sub')), parts along dimension 0, may hold values from 0 to 31, as said below
- parent_factor: float32 [8, 12, 256, 256], P(('parts', 'sub'), None, 'row'), parts along dimension 0, may hold values from -0.109375 to 0.109375
- parent_inverse: float32 [8, 256, 256], P(('parts', 'sub')), parts along dimension 0, may hold values from -6 to 6
- child_parent: int32 [8], P(('parts', 'sub')), parts along dimension 0, may hold values from 0 to 1
- child_pattern: int32 [8, 8], P(('parts', 'sub')), parts along dimension 0, may hold values from 0 to 11, as said below
- child_factor: float32 [8, 9, 256, 256], P(('parts', 'sub'), None, 'row'), parts along dimension 0, may hold values from -0.125 to 0.125
- child_inverse: float32 [8, 256, 256], P(('parts', 'sub')), parts along dimension 0, may hold values from -6 to 6
Outputs:
- parent_cov: float32 [8, 32, 256, 256], P(('parts', 'sub'), 'row'), parts along dimension 0
- parent_diag: float32 [8, 256, 256], P(('parts', 'sub')), parts along dimension 0
- child_cov: float32 [8, 32, 256, 256], P(('parts', 'sub'), 'row'), parts along dimension 0
- child_upper: float32 [8, 256, 256], P(('parts', 'sub')), parts along dimension 0
- child_diag: float32 [8, 256, 256], P(('parts', 'sub')), parts along dimension 0
There are 2 independent parts, one for each index of `parts`. A program takes and returns all parts, laid end to end along the dimension named above; each array names one. Nothing has to cross between parts.
Inputs may be any that keep to these rules, and one draw needn't show every extreme that they name: `parent_pattern`: each row holds distinct ancestor ids. `child_pattern`: each row holds distinct positions.
All inputs are finite; a program needn't handle non-finite values.
Results may differ from a plain program's by a relative error of at most 0.0001.
Values sent between devices are 32-bit elements; how exact they have to be, the bound alone decides.
No kernel may reach another device: no remote copies, remote signals or barrier semaphores. Data moves between devices by JAX's collectives and lax.ppermute only.
A program may use at most 192 MiB of HBM per device.

v0:
```python
import jax
import jax.numpy as jnp
from jax import lax
from jax.sharding import PartitionSpec as P

HIGH = lax.Precision.HIGHEST


def pick_rows(slot_list, targets):
    return (slot_list[:, None, :] == targets[None, :, None]).astype(jnp.float32)


def choose(selector, blocks):
    return jnp.einsum("jcp,jpxy->jcxy", selector, blocks, precision=HIGH)


def per_device(
    ancestor_cov,
    owner_slot,
    parent_pattern,
    parent_factor,
    parent_inverse,
    child_parent,
    child_pattern,
    child_factor,
    child_inverse,
):
    ancestor_count = owner_slot.shape[0]
    row_slots = ancestor_cov.shape[0]
    col_slots = ancestor_cov.shape[1]
    group_count = parent_pattern.shape[0]
    pattern_len = parent_pattern.shape[1]
    ancestor_ids = jnp.arange(ancestor_count, dtype=jnp.int32)
    match = (parent_pattern[:, :, None] == ancestor_ids[None, None, :]).astype(jnp.int32)
    slots = jnp.sum(match * owner_slot[None, None, :], axis=-1)
    row_ids = lax.axis_index("row") * row_slots + jnp.arange(row_slots, dtype=jnp.int32)
    col_ids = lax.axis_index("col") * col_slots + jnp.arange(col_slots, dtype=jnp.int32)
    parent_onehot = child_parent[:, None] == jnp.arange(group_count, dtype=jnp.int32)[None, :]
    kid_parent_slots = jnp.sum(
        parent_onehot[:, :, None].astype(jnp.int32) * slots[None, :, :], axis=1
    )
    rel_match = (
        child_pattern[:, :, None] == jnp.arange(pattern_len, dtype=jnp.int32)[None, None, :]
    ).astype(jnp.int32)
    kid_slots = jnp.sum(rel_match * kid_parent_slots[:, None, :], axis=-1)
    col_one = pick_rows(slots, col_ids)
    row_one = pick_rows(slots, row_ids)
    col_two = pick_rows(kid_slots, col_ids)
    row_two = pick_rows(kid_slots, row_ids)
    full_one, full_two = (
        lax.all_gather(parent_factor, "row", axis=2, tiled=True),
        lax.all_gather(child_factor, "row", axis=2, tiled=True),
    )
    wcol_one = choose(col_one, full_one)
    wrow_one = choose(row_one, full_one)
    lead = full_two[:, 0]
    wcol_two = choose(col_two, full_two[:, 1:])
    wrow_two = choose(row_two, full_two[:, 1:])
    mask_one = jnp.sum(row_one, axis=-1)
    mask_two = jnp.sum(row_two, axis=-1)
    parent_weight = parent_onehot.astype(jnp.float32)
    partial_one = jnp.einsum("icxy,jcyz->jixz", ancestor_cov, wcol_one, precision=HIGH)
    prod_one = lax.psum(partial_one, "col")
    parent_cov = -mask_one[:, :, None, None] * prod_one
    term_one = jnp.einsum("jixy,jixz->jyz", wrow_one, prod_one, precision=HIGH)
    parent_diag = parent_inverse - lax.psum(term_one, "row")
    kid_pcov = jnp.einsum("kj,jixy->kixy", parent_weight, parent_cov, precision=HIGH)
    partial_two = jnp.einsum("icxy,kcyz->kixz", ancestor_cov, wcol_two, precision=HIGH)
    prod_two = lax.psum(partial_two, "col")
    prod_two = prod_two + jnp.einsum("kixy,kyz->kixz", kid_pcov, lead, precision=HIGH)
    upper_part = jnp.einsum("kixy,kixz->kyz", kid_pcov, wrow_two, precision=HIGH)
    diag_part = jnp.einsum("kixy,kixz->kyz", wrow_two, prod_two, precision=HIGH)
    upper_sum, diag_sum = lax.psum((upper_part, diag_part), "row")
    kid_pdiag = jnp.einsum("kj,jxy->kxy", parent_weight, parent_diag, precision=HIGH)
    child_cov = -mask_two[:, :, None, None] * prod_two
    upper = jnp.einsum("kxy,kyz->kxz", kid_pdiag, lead, precision=HIGH) + upper_sum
    child_upper = -upper
    child_diag = child_inverse - jnp.einsum("kxy,kxz->kyz", lead, upper, precision=HIGH) - diag_sum
    return (parent_cov, parent_diag, child_cov, child_upper, child_diag)


def solution(mesh):
    in_specs = (
        P(("parts", "row"), "col", None, None),
        P("parts"),
        P(("parts", "sub"), None),
        P(("parts", "sub"), None, "row", None),
        P(("parts", "sub"), None, None),
        P(("parts", "sub")),
        P(("parts", "sub"), None),
        P(("parts", "sub"), None, "row", None),
        P(("parts", "sub"), None, None),
    )
    out_specs = (
        P(("parts", "sub"), "row", None, None),
        P(("parts", "sub"), None, None),
        P(("parts", "sub"), "row", None, None),
        P(("parts", "sub"), None, None),
        P(("parts", "sub"), None, None),
    )
    return jax.shard_map(
        per_device, mesh=mesh, in_specs=in_specs, out_specs=out_specs, check_vma=False
    )
```

profile of v0, /device:TPU:0, one launch (start us, length us, event | category | flops | bytes accessed | tf_op | source)
XLA Modules:
  0.0 643.6 jit_solution(5882674542085067443)
XLA Ops:
  11.1 35.0 %copy.54 = f32[8,16,256,256,1]{2,1,3,0,4:T(8,128)} copy(f32[8,16,256,256,1]{3,2,1,0,4:T(8,128)} %bitcast.92) | data formatting | bytes 67108864 | tf_op args[0]
  46.4 56.0 %all-gather.5.cloned.1.call-done = f32[2,9,256,256]{3,2,0,1:T(8,128)} async-done(((f32[2,9,64,256]{3,2,0,1:T(8,128)}), f32[2,9,256,256]{3,2,0,1:T(8,128)}) %all-gather.5.cloned.1.call-update) | async-done | bytes 4718608 | tf_op jit(solution)/shard_map/all_gather | solution.py:52
  102.3 2.6 slice.9
  107.1 5.8 fusion.12
  112.9 62.4 %fusion.22 = f32[2,8,256,256]{2,3,1,0:T(8,128)} fusion(f32[8,16,256,256,1]{2,1,3,0,4:T(8,128)} %copy.54, f32[2,16,256,256]{3,1,2,0:T(8,128)S(1)} %fusion.12), kind=kOutput, calls=%fused_computation.18 | convolution fusion | flops 51539607552 | bytes 46137344 | tf_op jit(solution)/shard_map/icxy,kcyz->kixz/dot_general | solution.py:68
  175.3 42.4 %all-gather.3.cloned.1.call-done = f32[2,12,256,256]{3,2,1,0:T(8,128)} async-done(((f32[2,12,64,256]{3,2,1,0:T(8,128)}), f32[2,12,256,256]{3,2,1,0:T(8,128)}) %all-gather.3.cloned.1.call-update) | async-done | bytes 6291472 | tf_op jit(solution)/shard_map/all_gather | solution.py:51
  217.7 10.7 %fusion.2 = f32[2,16,256,256]{3,1,2,0:T(8,128)S(1)} fusion(f32[2,12,256,256]{3,2,1,0:T(8,128)} %all-gather.3.cloned.1.call-done, s32[2,12]{1,0:T(2,128)S(1)} %copy.31, s32[16]{0:T(128)S(1)} %iota_add_fusion), kind=kOutput, calls=%fused_computation.2 | convolution fusion | flops 301990272 | bytes 14680224 | tf_op jit(solution)/shard_map/jcp,jpxy->jcxy/dot_general | solution.py:14
  228.4 62.5 %fusion.19 = f32[2,8,256,256]{2,3,1,0:T(8,128)} fusion(f32[8,16,256,256,1]{2,1,3,0,4:T(8,128)} %copy.54, f32[2,16,256,256]{3,1,2,0:T(8,128)S(1)} %fusion.2), kind=kOutput, calls=%fused_computation.17 | convolution fusion | flops 51539607552 | bytes 46137344 | tf_op jit(solution)/shard_map/icxy,jcyz->jixz/dot_general | solution.py:62
  291.8 8.7 %fusion.14 = f32[2,8,256,256]{3,1,2,0:T(8,128)} fusion(f32[2,8,256,256]{3,2,0,1:T(8,128)} %copy-done, s32[2,8]{1,0:T(2,128)S(1)} %copy-done.12, s32[8]{0:T(128)S(1)} %iota_add_fusion.1), kind=kOutput, calls=%fused_computation.14 | convolution fusion | flops 100663424 | bytes 8388704 | tf_op jit(solution)/shard_map/jcp,jpxy->jcxy/dot_general | solution.py:14
  300.5 7.4 %fusion = f32[2,8,256,256]{3,1,2,0:T(8,128)} fusion(f32[2,12,256,256]{3,2,1,0:T(8,128)S(1)} %bitcast.91, s32[2,12]{1,0:T(2,128)S(1)} %copy.31, s32[8]{0:T(128)S(1)} %iota_add_fusion.1), kind=kOutput, calls=%fused_computation | convolution fusion | flops 150995136 | bytes 10485888 | tf_op jit(solution)/shard_map/jcp,jpxy->jcxy/dot_general | solution.py:14
  307.8 180.0 %all-reduce.7.cloned.1.call-done = (f32[2,8,256,256]{2,3,1,0:T(8,128)}, f32[2,8,256,256]{2,3,1,0:T(8,128)}) async-done(((f32[2,8,256,256]{2,3,1,0:T(8,128)}, f32[2,8,256,256]{2,3,1,0:T(8,128)}), (f32[2,8,256,256]{2,3,1,0:T(8,128)}, f32[2,8,256,256]{2,3,1,0:T(8,128)})) %all-reduce.7.cloned.1.call-update) | async-done | bytes 8388624 | tf_op jit(solution)/shard_map/psum | solution.py:63
  487.9 5.4 copy.59
  493.3 4.7 broadcast_multiply_fusion.1
  498.0 7.3 %copy.36 = f32[2,8,256,256]{3,0,2,1:T(2,128)} copy(f32[2,8,256,256]{2,3,1,0:T(8,128)} %broadcast_multiply_fusion.1) | data formatting | bytes 8388608 | tf_op jit(solution)/shard_map/mul | solution.py:64
  505.3 10.2 %fusion.54 = f32[2,8,256,256]{3,0,2,1:T(2,128)S(1)} fusion(f32[2,8,256,256]{3,0,2,1:T(2,128)} %copy.36, s32[2]{0:T(128)S(1)} %copy-done.14), kind=kOutput, calls=%fused_computation.60 | convolution fusion | flops 25165828 | bytes 8388616 | tf_op jit(solution)/shard_map/kj,jixy->kixy/dot_general | solution.py:67
  515.5 7.9 %broadcast_multiply_fusion = (f32[2,8,256,256]{2,3,1,0:T(8,128)}, f32[2,8,256,256]{2,3,1,0:T(8,128)}) fusion(f32[2,8]{1,0:T(2,128)S(1)} %neg.20, f32[2,8,256,256]{2,3,1,0:T(8,128)S(1)} %copy-done.4, f32[2,9,256,256]{3,2,0,1:T(8,128)} %all-gather.5.cloned.1.call-done, f32[2,8,256,256]{3,0,2,1:T(2,128)S(1)} %fusion.54), kind=kOutput, calls=%fused_computation.19 | convolution fusion | flops 3223322624 | bytes 17301568 | tf_op jit(solution)/shard_map/kixy,kyz->kixz/dot_general | solution.py:70
  523.4 5.8 copy.76
  529.3 12.9 %fusion.27 = f32[2,256,256]{2,1,0:T(8,128)} fusion(f32[2,8,256,256]{3,1,2,0:T(8,128)} %fusion.14, f32[2,8,256,256]{3,0,2,1:T(2,128)} %copy-done.1), kind=kOutput, calls=%fused_computation.26 | convolution fusion | flops 3221225472 | bytes 8912896 | tf_op jit(solution)/shard_map/kixy,kixz->kyz/dot_general | solution.py:71
  542.2 8.0 %convolution_bitcast_fusion = f32[2,256,256]{1,2,0:T(8,128)} fusion(f32[2,8,256,256]{3,1,2,0:T(8,128)S(1)} %copy-done.2, f32[2,8,256,256]{3,1,2,0:T(8,128)S(1)} %copy-done.3), kind=kOutput, calls=%fused_computation.21 | convolution fusion | flops 3221225472 | bytes 8912896 | tf_op jit(solution)/shard_map/kixy,kixz->kyz/dot_general | solution.py:72
  550.3 7.9 %convolution_bitcast_fusion.2 = f32[2,256,256]{2,1,0:T(8,128)} fusion(f32[2,8,256,256]{3,1,2,0:T(8,128)S(1)} %copy-done.5, f32[2,8,256,256]{3,1,2,0:T(8,128)S(1)} %copy-done.6), kind=kOutput, calls=%fused_computation.27 | convolution fusion | flops 3221225472 | bytes 8912896 | tf_op jit(solution)/shard_map/jixy,jixz->jyz/dot_general | solution.py:65
  558.4 5.4 copy.47
  563.8 5.6 copy.48
  569.4 59.2 %all-reduce.5.cloned.1.call-done = (f32[2,256,256]{2,1,0:T(8,128)}, f32[2,256,256]{2,1,0:T(8,128)}, f32[2,256,256]{1,2,0:T(8,128)}) async-done(((f32[2,256,256]{2,1,0:T(8,128)}, f32[2,256,256]{2,1,0:T(8,128)}, f32[2,256,256]{1,2,0:T(8,128)}), (f32[2,256,256]{2,1,0:T(8,128)}, f32[2,256,256]{2,1,0:T(8,128)}, f32[2,256,256]{1,2,0:T(8,128)})) %all-reduce.5.cloned.1.call-update) | async-done | bytes 1572880 | tf_op jit(solution)/shard_map/psum | solution.py:66
  631.1 2.7 fusion.60
  (67 shorter events, 12.8 us)
Async XLA Ops:
  7.2 3.3 copy-start.15
  7.2 3.4 copy-start.17
  7.2 3.8 copy-start.13
  7.2 95.1 %all-gather.5.cloned.1.call-start = ((), (), s32[]{:S(2)}) async-start(), calls=%async_computation.1 | async-start | bytes 5898240 | tf_op jit(solution)/shard_map/all_gather | solution.py:52
  9.7 208.0 %all-gather.3.cloned.1.call-start = ((), (), s32[]{:S(2)}) async-start(), calls=%async_computation | async-start | bytes 7864320 | tf_op jit(solution)/shard_map/all_gather | solution.py:51
  10.4 477.4 %all-reduce.7.cloned.1.call-start = ((), (), s32[]{:S(2)}) async-start(), calls=%async_computation.3 | async-start | bytes 16777216 | tf_op jit(solution)/shard_map/psum | solution.py:63
  11.1 35.0 %copy-start.16 = (s32[2,8]{1,0:T(2,128)S(1)}, s32[2,8]{1,0:T(2,128)}, u32[]{:S(2)}) copy-start(s32[2,8]{1,0:T(2,128)} %param.15) | copy-start | bytes 196
  46.3 58.6 %copy-start.11 = (s32[2,8]{1,0:T(2,128)}, s32[2,8]{1,0:T(2,128)S(1)}, u32[]{:S(2)}) copy-start(s32[2,8]{1,0:T(2,128)S(1)} %select_reduce_fusion) | copy-start | bytes 196
  105.0 2.1 copy-start
  290.9 0.7 copy-start.12
  290.9 9.6 %slice-start = ((s8[6291456]{0:T(1024)(128)(4,1)}), s8[2097152]{0:T(1024)(128)(4,1)S(1)}, s32[]{:S(2)}) async-start(s8[6291456]{0:T(1024)(128)(4,1)} %bitcast.90), calls=%async_computation.4 | async-start | bytes 4194304
  291.0 337.6 %all-reduce.5.cloned.1.call-start = ((), (), s32[]{:S(2)}) async-start(), calls=%async_computation.2 | async-start | bytes 3145728 | tf_op jit(solution)/shard_map/psum | solution.py:66
  291.0 9.5 %slice-start.1 = ((s8[6291456]{0:T(1024)(128)(4,1)}), s8[4194304]{0:T(1024)(128)(4,1)S(1)}, s32[]{:S(2)}) async-start(s8[6291456]{0:T(1024)(128)(4,1)} %bitcast.90), calls=%async_computation.5 | async-start | bytes 8388608
  498.0 7.3 %copy-start.14 = (s32[2]{0:T(128)S(1)}, s32[2]{0:T(128)}, u32[]{:S(2)}) copy-start(s32[2]{0:T(128)} %param.14) | copy-start | bytes 28
  505.3 10.3 %copy-start.4 = (f32[2,8,256,256]{2,3,1,0:T(8,128)S(1)}, f32[2,8,256,256]{2,3,1,0:T(8,128)}, u32[]{:S(2)}) copy-start(f32[2,8,256,256]{2,3,1,0:T(8,128)} %get-tuple-element.19) | copy-start | bytes 12582916
  515.5 7.9 %copy-start.1 = (f32[2,8,256,256]{3,0,2,1:T(2,128)}, f32[2,8,256,256]{3,0,2,1:T(2,128)S(1)}, u32[]{:S(2)}) copy-start(f32[2,8,256,256]{3,0,2,1:T(2,128)S(1)} %fusion.54) | copy-start | bytes 12582916
  529.3 13.0 %copy-start.2 = (f32[2,8,256,256]{3,1,2,0:T(8,128)S(1)}, f32[2,8,256,256]{3,1,2,0:T(8,128)}, u32[]{:S(2)}) copy-start(f32[2,8,256,256]{3,1,2,0:T(8,128)} %fusion.14) | copy-start | bytes 12582916
  529.3 12.9 %copy-start.3 = (f32[2,8,256,256]{3,1,2,0:T(8,128)S(1)}, f32[2,8,256,256]{3,1,2,0:T(8,128)}, u32[]{:S(2)}) copy-start(f32[2,8,256,256]{3,1,2,0:T(8,128)} %copy.76) | copy-start | bytes 12582916
  542.2 8.0 %copy-start.5 = (f32[2,8,256,256]{3,1,2,0:T(8,128)S(1)}, f32[2,8,256,256]{3,1,2,0:T(8,128)}, u32[]{:S(2)}) copy-start(f32[2,8,256,256]{3,1,2,0:T(8,128)} %fusion) | copy-start | bytes 12582916
  542.2 8.0 %copy-start.6 = (f32[2,8,256,256]{3,1,2,0:T(8,128)S(1)}, f32[2,8,256,256]{3,1,2,0:T(8,128)}, u32[]{:S(2)}) copy-start(f32[2,8,256,256]{3,1,2,0:T(8,128)} %copy.59) | copy-start | bytes 12582916
  550.3 7.9 %copy-start.10 = (f32[2,256,256]{2,1,0:T(8,128)S(1)}, f32[2,256,256]{2,1,0:T(8,128)}, u32[]{:S(2)}) copy-start(f32[2,256,256]{2,1,0:T(8,128)} %param.17) | copy-start | bytes 1572868
  563.8 64.8 %copy-start.8 = (f32[2,256,256]{2,1,0:T(8,128)S(1)}, f32[2,256,256]{2,1,0:T(8,128)}, u32[]{:S(2)}) copy-start(f32[2,256,256]{2,1,0:T(8,128)} %param.13) | copy-start | bytes 1572868
  628.6 5.2 copy-start.9
  629.8 7.1 %copy-start.7 = (f32[2,256,256]{2,1,0:T(8,128)}, f32[2,256,256]{2,1,0:T(8,128)S(1)}, u32[]{:S(2)}) copy-start(f32[2,256,256]{2,1,0:T(8,128)S(1)} %sub.9) | copy-start | bytes 1572868
Sparse Core Ops, SparseCore 0:
  10.2 92.0 all-gather.4
  103.9 113.7 all-gather.2
  291.1 196.7 all-reduce.6
  558.3 70.2 all-reduce.4
where the time goes:
time: 650 us; the launch traced here: 644 us
  waiting for transfers between devices  338 us (52%)
  matrix products  210 us (32%)
  local copies, waits for them, and re-layouts  73.5 us (11%)
  between operations  14.3 us (2%)
  other arithmetic  6.93 us (1%)
    psum x1, waiting for transfers between devices, per_device(): prod_one = lax.psum(partial_one, 'col')  180 us
    dot_general x1, matrix products, per_device(): jnp.einsum('icxy,jcyz->jixz', ancestor_cov, wcol_one, precision=HIGH)  62.5 us
    dot_general x1, matrix products, per_device(): jnp.einsum('icxy,kcyz->kixz', ancestor_cov, wcol_two, precision=HIGH)  62.4 us
    psum x1, waiting for transfers between devices, per_device(): parent_diag = parent_inverse - lax.psum(term_one, 'row')  59.2 us
    all_gather x1, waiting for transfers between devices, per_device(): lax.all_gather(child_factor, 'row', axis=2, tiled=True)  56 us
    unnamed x47, local copies, waits for them, and re-layouts  52.2 us
    all_gather x1, waiting for transfers between devices, per_device(): lax.all_gather(parent_factor, 'row', axis=2, tiled=True)  42.4 us
    dot_general x4, matrix products, choose(): return jnp.einsum('jcp,jpxy->jcxy', selector, blocks, precision=HIGH)  32.5 us
  transfers between devices with their start and end apart: 4, of which 4 were waited for; matrix products, arithmetic and copies ran while one was open for 21% of the time, Pallas kernels for 0%

commit v1 on v0

--- a/solution.py
+++ b/solution.py
@@ -63,7 +63,7 @@
     prod_one = lax.psum(partial_one, "col")
     parent_cov = -mask_one[:, :, None, None] * prod_one
     term_one = jnp.einsum("jixy,jixz->jyz", wrow_one, prod_one, precision=HIGH)
-    parent_diag = parent_inverse - lax.psum(term_one, "row")
+    parent_diag = parent_inverse - jnp.sum(lax.all_gather(term_one, "row"), axis=0)
     kid_pcov = jnp.einsum("kj,jixy->kixy", parent_weight, parent_cov, precision=HIGH)
     partial_two = jnp.einsum("icxy,kcyz->kixz", ancestor_cov, wcol_two, precision=HIGH)
     prod_two = lax.psum(partial_two, "col")

time: 650 us -> 730 us (1.12)
  waiting for transfers between devices: 338 us -> 410 us
    all_gather x1, waiting for transfers between devices: 56 us -> 114 us  [per_device(): lax.all_gather(child_factor, 'row', axis=2, tiled=True)]
    all_gather x1, waiting for transfers between devices: 42.4 us -> 80.3 us  [per_device(): lax.all_gather(parent_factor, 'row', axis=2, tiled=True)]
    psum x1, waiting for transfers between devices: 59.2 us -> 38.5 us  [per_device(): upper_sum, diag_sum = lax.psum((upper_part, diag_part), 'row')]
    dot_general x1, matrix products: 62.5 us -> 72.5 us  [per_device(): jnp.einsum('icxy,jcyz->jixz', ancestor_cov, wcol_one, precision=HIGH)]
    unnamed x47 -> x42, local copies, waits for them, and re-layouts: 52.2 us -> 54.5 us
  transfers between devices with their start and end apart: 4 -> 5, of which waited for: 4 -> 4; matrix products, arithmetic and copies ran while one was open for 21% -> 26% of each run, Pallas kernels for 0% -> 0%
where the time goes in v1:
time: 730 us; the launch traced here: 725 us
  waiting for transfers between devices  410 us (56%)
  matrix products  217 us (30%)
  local copies, waits for them, and re-layouts  75.3 us (10%)
  between operations  14.2 us (2%)
  other arithmetic  7.89 us (1%)
    psum x1, waiting for transfers between devices, per_device(): prod_one = lax.psum(partial_one, 'col')  177 us
    all_gather x1, waiting for transfers between devices, per_device(): lax.all_gather(child_factor, 'row', axis=2, tiled=True)  114 us
    all_gather x1, waiting for transfers between devices, per_device(): lax.all_gather(parent_factor, 'row', axis=2, tiled=True)  80.3 us
    dot_general x1, matrix products, per_device(): jnp.einsum('icxy,jcyz->jixz', ancestor_cov, wcol_one, precision=HIGH)  72.5 us
    dot_general x1, matrix products, per_device(): jnp.einsum('icxy,kcyz->kixz', ancestor_cov, wcol_two, precision=HIGH)  63.4 us
    unnamed x42, local copies, waits for them, and re-layouts  54.5 us
    psum x1, waiting for transfers between devices, per_device(): upper_sum, diag_sum = lax.psum((upper_part, diag_part), 'row')  38.5 us
    dot_general x4, matrix products, choose(): return jnp.einsum('jcp,jpxy->jcxy', selector, blocks, precision=HIGH)  29.5 us
  transfers between devices with their start and end apart: 5, of which 4 were waited for; matrix products, arithmetic and copies ran while one was open for 26% of the time, Pallas kernels for 0%

profile of v1, /device:TPU:0, one launch (start us, length us, event | category | flops | bytes accessed | tf_op | source)
XLA Modules:
  0.0 724.7 jit_solution(1218453191620871023)
XLA Ops:
  7.2 3.4 copy.54
  13.7 34.9 %copy.71 = f32[8,16,256,256,1]{2,1,3,0,4:T(8,128)} copy(f32[8,16,256,256,1]{3,2,1,0,4:T(8,128)} %bitcast.93) | data formatting | bytes 67108864 | tf_op args[0]
  48.9 114.3 %all-gather.7.cloned.1.call-done = f32[2,9,256,256]{3,1,2,0:T(8,128)} async-done(((f32[2,9,64,256]{3,1,2,0:T(8,128)}), f32[2,9,256,256]{3,1,2,0:T(8,128)}) %all-gather.7.cloned.1.call-update) | async-done | bytes 4718608 | tf_op jit(solution)/shard_map/all_gather | solution.py:52
  163.2 6.2 fusion.10
  169.4 63.4 %fusion.18 = f32[2,8,256,256]{2,3,1,0:T(8,128)} fusion(f32[8,16,256,256,1]{2,1,3,0,4:T(8,128)} %copy.71, f32[2,16,256,256]{3,1,2,0:T(8,128)S(1)} %fusion.10), kind=kOutput, calls=%fused_computation.14 | convolution fusion | flops 51539607552 | bytes 46137344 | tf_op jit(solution)/shard_map/icxy,kcyz->kixz/dot_general | solution.py:68
  232.8 80.3 %all-gather.5.cloned.1.call-done = f32[2,12,256,256]{3,1,2,0:T(8,128)} async-done(((f32[2,12,64,256]{3,1,2,0:T(8,128)}), f32[2,12,256,256]{3,1,2,0:T(8,128)}) %all-gather.5.cloned.1.call-update) | async-done | bytes 6291472 | tf_op jit(solution)/shard_map/all_gather | solution.py:51
  313.2 6.8 fusion.35
  320.0 72.5 %fusion.15 = f32[2,8,256,256]{2,3,1,0:T(8,128)} fusion(f32[8,16,256,256,1]{2,1,3,0,4:T(8,128)} %copy.71, f32[2,16,256,256]{3,1,2,0:T(8,128)S(1)} %fusion.35), kind=kOutput, calls=%fused_computation.13 | convolution fusion | flops 51539607552 | bytes 46137344 | tf_op jit(solution)/shard_map/icxy,jcyz->jixz/dot_general | solution.py:62
  396.0 8.1 %fusion.8 = f32[2,8,256,256]{3,1,2,0:T(8,128)} fusion(f32[2,9,256,256]{3,1,2,0:T(8,128)} %all-gather.7.cloned.1.call-done, s32[2,8]{1,0:T(2,128)S(1)} %copy-done.11, s32[8]{0:T(128)S(1)} %iota_add_fusion.1), kind=kOutput, calls=%fused_computation.8 | convolution fusion | flops 100663424 | bytes 8388704 | tf_op jit(solution)/shard_map/jcp,jpxy->jcxy/dot_general | solution.py:14
  404.1 8.4 %fusion.43 = f32[2,8,256,256]{3,1,2,0:T(8,128)} fusion(f32[2,12,256,256]{3,1,2,0:T(8,128)} %all-gather.5.cloned.1.call-done, s32[2,12]{1,0:T(2,128)S(1)} %copy.47, s32[8]{0:T(128)S(1)} %iota_add_fusion.1), kind=kOutput, calls=%fused_computation.48 | convolution fusion | flops 150995136 | bytes 10485888 | tf_op jit(solution)/shard_map/jcp,jpxy->jcxy/dot_general | solution.py:14
  412.5 177.0 %all-reduce.7.cloned.1.call-done = (f32[2,8,256,256]{2,3,1,0:T(8,128)}, f32[2,8,256,256]{2,3,1,0:T(8,128)}) async-done(((f32[2,8,256,256]{2,3,1,0:T(8,128)}, f32[2,8,256,256]{2,3,1,0:T(8,128)}), (f32[2,8,256,256]{2,3,1,0:T(8,128)}, f32[2,8,256,256]{2,3,1,0:T(8,128)})) %all-reduce.7.cloned.1.call-update) | async-done | bytes 8388624 | tf_op jit(solution)/shard_map/psum | solution.py:63
  589.5 5.4 copy.75
  594.9 5.0 broadcast_multiply_fusion.1
  601.2 7.9 %convolution_bitcast_fusion.2 = f32[2,256,256]{2,1,0:T(8,128)} fusion(f32[2,8,256,256]{3,1,2,0:T(8,128)S(1)} %copy-done.4, f32[2,8,256,256]{3,1,2,0:T(8,128)S(1)} %copy-done.5), kind=kOutput, calls=%fused_computation.23 | convolution fusion | flops 3221225472 | bytes 8912896 | tf_op jit(solution)/shard_map/jixy,jixz->jyz/dot_general | solution.py:65
  609.1 7.2 copy.56
  616.4 10.3 %fusion.52 = f32[2,8,256,256]{3,0,2,1:T(2,128)S(1)} fusion(f32[2,8,256,256]{3,0,2,1:T(2,128)} %copy.56, s32[2]{0:T(128)S(1)} %copy-done.13), kind=kOutput, calls=%fused_computation.58 | convolution fusion | flops 25165828 | bytes 8388616 | tf_op jit(solution)/shard_map/kj,jixy->kixy/dot_general | solution.py:67
  626.7 6.5 broadcast_multiply_fusion
  633.2 5.6 copy.64
  638.8 11.2 %convolution_bitcast_fusion = f32[2,256,256]{1,2,0:T(8,128)} fusion(f32[2,8,256,256]{3,1,2,0:T(8,128)} %fusion.8, f32[2,8,256,256]{3,1,2,0:T(8,128)} %copy.64), kind=kOutput, calls=%fused_computation.17 | convolution fusion | flops 3221225472 | bytes 8912896 | tf_op jit(solution)/shard_map/kixy,kixz->kyz/dot_general | solution.py:72
  650.1 9.6 %fusion.23 = f32[2,256,256]{2,1,0:T(8,128)} fusion(f32[2,8,256,256]{3,1,2,0:T(8,128)S(1)} %copy-done.2, f32[2,8,256,256]{3,0,2,1:T(2,128)S(1)} %copy-done.1), kind=kOutput, calls=%fused_computation.22 | convolution fusion | flops 3221225472 | bytes 8912896 | tf_op jit(solution)/shard_map/kixy,kixz->kyz/dot_general | solution.py:71
  659.9 5.4 copy.66
  665.2 5.4 copy.67
  673.9 38.5 %all-reduce.5.cloned.1.call-done = (f32[2,256,256]{2,1,0:T(8,128)}, f32[2,256,256]{1,2,0:T(8,128)}) async-done(((f32[2,256,256]{2,1,0:T(8,128)}, f32[2,256,256]{1,2,0:T(8,128)}), (f32[2,256,256]{2,1,0:T(8,128)}, f32[2,256,256]{1,2,0:T(8,128)})) %all-reduce.5.cloned.1.call-update) | async-done | bytes 1048592 | tf_op jit(solution)/shard_map/psum | solution.py:73
  712.4 2.5 fusion.58
  (65 shorter events, 14.5 us)
Async XLA Ops:
  7.2 3.6 copy-start.7
  7.2 156.0 %all-gather.7.cloned.1.call-start = ((), (), s32[]{:S(2)}) async-start(), calls=%async_computation.1 | async-start | bytes 10485760 | tf_op jit(solution)/shard_map/all_gather | solution.py:52
  10.7 2.4 copy-start.12
  10.7 2.5 copy-start.14
  10.7 2.6 copy-start.16
  10.7 302.5 %all-gather.5.cloned.1.call-start = ((), (), s32[]{:S(2)}) async-start(), calls=%async_computation | async-start | bytes 10485760 | tf_op jit(solution)/shard_map/all_gather | solution.py:51
  13.0 576.5 %all-reduce.7.cloned.1.call-start = ((), (), s32[]{:S(2)}) async-start(), calls=%async_computation.4 | async-start | bytes 16777216 | tf_op jit(solution)/shard_map/psum | solution.py:63
  13.7 34.9 %copy-start.15 = (s32[2,8]{1,0:T(2,128)S(1)}, s32[2,8]{1,0:T(2,128)}, u32[]{:S(2)}) copy-start(s32[2,8]{1,0:T(2,128)} %param.15) | copy-start | bytes 196
  48.9 120.5 %copy-start.10 = (s32[2,8]{1,0:T(2,128)}, s32[2,8]{1,0:T(2,128)S(1)}, u32[]{:S(2)}) copy-start(s32[2,8]{1,0:T(2,128)S(1)} %select_reduce_fusion) | copy-start | bytes 196
  392.6 0.7 copy-start.11
  392.6 278.1 %all-gather.9.cloned.1.call-start = ((), (), s32[]{:S(2)}) async-start(), calls=%async_computation.2 | async-start | bytes 2621440 | tf_op jit(solution)/shard_map/all_gather | solution.py:66
  594.9 5.0 copy-start.4
  594.9 6.2 copy-start.5
  609.1 7.3 %copy-start.13 = (s32[2]{0:T(128)S(1)}, s32[2]{0:T(128)}, u32[]{:S(2)}) copy-start(s32[2]{0:T(128)} %param.14) | copy-start | bytes 28
  609.1 103.3 %all-reduce.5.cloned.1.call-start = ((), (), s32[]{:S(2)}) async-start(), calls=%async_computation.3 | async-start | bytes 2097152 | tf_op jit(solution)/shard_map/psum | solution.py:73
  616.4 10.3 %copy-start.3 = (f32[2,8,256,256]{2,3,1,0:T(8,128)S(1)}, f32[2,8,256,256]{2,3,1,0:T(8,128)}, u32[]{:S(2)}) copy-start(f32[2,8,256,256]{2,3,1,0:T(8,128)} %get-tuple-element.23) | copy-start | bytes 12582916
  626.7 6.5 copy-start
  638.8 11.2 %copy-start.1 = (f32[2,8,256,256]{3,0,2,1:T(2,128)S(1)}, f32[2,8,256,256]{3,0,2,1:T(2,128)}, u32[]{:S(2)}) copy-start(f32[2,8,256,256]{3,0,2,1:T(2,128)} %copy-done) | copy-start | bytes 12582916
  638.8 11.2 %copy-start.2 = (f32[2,8,256,256]{3,1,2,0:T(8,128)S(1)}, f32[2,8,256,256]{3,1,2,0:T(8,128)}, u32[]{:S(2)}) copy-start(f32[2,8,256,256]{3,1,2,0:T(8,128)} %fusion.8) | copy-start | bytes 12582916
  650.0 9.6 %copy-start.9 = (f32[2,256,256]{2,1,0:T(8,128)S(1)}, f32[2,256,256]{2,1,0:T(8,128)}, u32[]{:S(2)}) copy-start(f32[2,256,256]{2,1,0:T(8,128)} %param.17) | copy-start | bytes 1572868
  665.2 7.2 copy-start.8
  672.5 45.4 %copy-start.6 = (f32[2,256,256]{2,1,0:T(8,128)}, f32[2,256,256]{2,1,0:T(8,128)S(1)}, u32[]{:S(2)}) copy-start(f32[2,256,256]{2,1,0:T(8,128)S(1)} %sub.9) | copy-start | bytes 1572868
Sparse Core Ops, SparseCore 0:
  10.8 152.3 all-gather.6
  165.3 147.8 all-gather.4
  392.7 196.7 all-reduce.6
  609.2 46.2 all-gather.8
  659.8 52.5 all-reduce.4
